TPU v7x, 32 devices: a whole 2x2x4 slice. The times are simulated.
32 devices in a mesh: groups: 2 (over y), gx: 4 (over z), gy: 4 (over x, core).
Axes of the slice: x: 2, y: 2, z: 4, core: 2. Of those that a mesh axis runs over, the one named last changes fastest.
Arguments:
- mean_field: float32 [3, 8, 8, 512], P(None, ('groups', 'gx'), None, 'gy'), parts along dimension 1, may hold values from -6 to 6
- modes: float32 [32, 3, 8, 8, 512], P(None, None, ('groups', 'gx'), None, 'gy'), parts along dimension 2, may hold values from -6 to 6
- samples: float32 [32, 32768], P(None, ('groups', 'gx', 'gy')), parts along dimension 1, may hold values from -41 to 41, as said below
Outputs:
- mean_rate: float32 [3, 8, 8, 512], P(None, ('groups', 'gx'), None, 'gy'), parts along dimension 1
- modes_tendency: float32 [32, 3, 8, 8, 512], P(None, None, ('groups', 'gx'), None, 'gy'), parts along dimension 2
- sample_rate: float32 [32, 32768], P(None, ('groups', 'gx', 'gy')), parts along dimension 1
There are 2 independent parts, one for each index of `groups`. A program takes and returns all parts, laid end to end along the dimension named above; each array names one. Nothing has to cross between parts.
Inputs may be any that keep to these rules, and one draw needn't show every extreme that they name: `samples`: samples of different modes have different spreads and are correlated; their distribution is skewed.
All inputs are finite; a program needn't handle non-finite values.
Results may differ from a plain program's by a relative error of at most 0.00012.
Values sent between devices are 32-bit elements; how exact they have to be, the bound alone decides.
A program may use at most 128 MiB of HBM per device.

v0:
```python
import math

import jax
import jax.numpy as jnp
from jax import lax
from jax.sharding import PartitionSpec as P

top_degree = lax.Precision.HIGHEST
viscosity = 0.2


def with_halo(cells, sides, width):
    for axis, dim in sides:
        count = lax.axis_size(axis)
        head = lax.slice_in_dim(cells, 0, width, axis=dim)
        tail = lax.slice_in_dim(cells, cells.shape[dim] - width, cells.shape[dim], axis=dim)
        cells = jnp.concatenate(
            [
                lax.ppermute(tail, axis, [(i, (i + 1) % count) for i in range(count)]),
                cells,
                lax.ppermute(head, axis, [((i + 1) % count, i) for i in range(count)]),
            ],
            axis=dim,
        )
    return cells


def derivatives(padded):
    widened = jnp.pad(padded, ((0, 0), (0, 0), (0, 0), (1, 1), (0, 0)))
    centre = widened[:, :, 1:-1, 1:-1, 1:-1]
    x_plus = widened[:, :, 2:, 1:-1, 1:-1]
    x_minus = widened[:, :, :-2, 1:-1, 1:-1]
    z_plus = widened[:, :, 1:-1, 2:, 1:-1]
    z_minus = widened[:, :, 1:-1, :-2, 1:-1]
    y_plus = widened[:, :, 1:-1, 1:-1, 2:]
    y_minus = widened[:, :, 1:-1, 1:-1, :-2]
    gradient = jnp.stack(
        [(x_plus - x_minus) * 0.5, (y_plus - y_minus) * 0.5, (z_plus - z_minus) * 0.5], axis=2
    )
    laplace = x_plus + x_minus + y_plus + y_minus + z_plus + z_minus - 6.0 * centre
    return (centre, gradient, laplace)


def into_blocks(array, width):
    shape = array.shape
    pieces = shape[-1] // width
    return jnp.moveaxis(array.reshape(shape[:-1] + (pieces, width)), -2, 0)


def triple_products(basis_matrix, basis_slopes, width):
    number = basis_matrix.shape[0]

    def triple_step_forward(summed, pieces):
        value_entries, slope_arrays = pieces
        weighted_terms = jnp.einsum(
            "rsf,nsbf->rnbf", value_entries, slope_arrays, precision=top_degree
        )
        return (
            summed
            + jnp.einsum("kdc,ildc->ikl", value_entries, weighted_terms, precision=top_degree),
            None,
        )

    summed, _ = lax.scan(
        triple_step_forward,
        jnp.zeros((number, number, number), jnp.float32),
        (into_blocks(basis_matrix, width), into_blocks(basis_slopes, width)),
    )
    return summed


def mode_advection(folded, basis_matrix, basis_slopes, width):
    number = basis_matrix.shape[0]

    def mode_step_forward(carried_over, pieces):
        value_entries, slope_arrays = pieces
        velocity_field = jnp.einsum("ikl,kdc->ildc", folded, value_entries, precision=top_degree)
        return (
            carried_over,
            jnp.einsum("nyfu,ytfu->ntu", velocity_field, slope_arrays, precision=top_degree),
        )

    _, stacked = lax.scan(
        mode_step_forward,
        jnp.zeros((), jnp.float32),
        (into_blocks(basis_matrix, width), into_blocks(basis_slopes, width)),
    )
    return jnp.moveaxis(stacked, 0, 2).reshape(number, 3, -1)


def third_moment(value_entries, width):
    number = value_entries.shape[0]

    def third_step_forward(summed, piece):
        pairs = (piece[:, None, :] * piece[None, :, :]).reshape(number * number, -1)
        return (
            summed
            + jnp.dot(piece, pairs.T, precision=top_degree, preferred_element_type=jnp.float32),
            None,
        )

    summed, _ = lax.scan(
        third_step_forward,
        jnp.zeros((number, number * number), jnp.float32),
        into_blocks(value_entries, width),
    )
    return summed.reshape(number, number, number)


def sample_response(centred, linear_projection, triple_proj, covariance, width):
    number = centred.shape[0]
    flat_proj = triple_proj.reshape(number, number * number)
    offset = jnp.sum(triple_proj * covariance[None], axis=(1, 2))

    def sample_step_forward(carried_over, piece):
        pairs = (piece[:, None, :] * piece[None, :, :]).reshape(number * number, -1)
        result = jnp.dot(
            linear_projection.T, piece, precision=top_degree, preferred_element_type=jnp.float32
        )
        result = result - jnp.dot(
            flat_proj, pairs, precision=top_degree, preferred_element_type=jnp.float32
        )
        return (carried_over, result + offset[:, None])

    _, stacked = lax.scan(
        sample_step_forward, jnp.zeros((), jnp.float32), into_blocks(centred, width)
    )
    return jnp.moveaxis(stacked, 0, 1).reshape(number, -1)


def body(mean_field, modes, samples):
    number = modes.shape[0]
    fields = jnp.concatenate([mean_field[None], modes], axis=0)
    padded = with_halo(fields, (("gx", 2), ("gy", 4)), 1)
    centre, gradient, laplace = derivatives(padded)
    grid_samples = centre.shape[2] * centre.shape[3] * centre.shape[4]
    members = lax.axis_size("gx") * lax.axis_size("gy")
    total_cells = grid_samples * members
    basis_matrix = centre[1:].reshape(number, 3, grid_samples)
    mean_flat = centre[0].reshape(3, grid_samples)
    basis_slopes = gradient[1:].reshape(number, 3, 3, grid_samples)
    mean_grad = gradient[0].reshape(3, 3, grid_samples)
    modes_lap = laplace[1:].reshape(number, 3, grid_samples)
    mean_lap = laplace[0].reshape(3, grid_samples)
    linear_term = (
        -jnp.einsum("dc,kedc->kec", mean_flat, basis_slopes, precision=top_degree)
        - jnp.einsum("kdc,edc->kec", basis_matrix, mean_grad, precision=top_degree)
        + viscosity * modes_lap
    )
    cell_width = math.gcd(grid_samples, 128)
    linear_local_part = jnp.einsum("pxa,qxa->pq", linear_term, basis_matrix, precision=top_degree)
    proj_local = triple_products(basis_matrix, basis_slopes, cell_width)
    sample_local = samples.shape[1]
    sample_total = sample_local * members
    sample_width = math.gcd(sample_local, 256)
    average = lax.psum(jnp.sum(samples, axis=1), ("gx", "gy")) / sample_total
    centred = samples - average[:, None]
    second_local = jnp.dot(
        centred, centred.T, precision=top_degree, preferred_element_type=jnp.float32
    )
    third_local = third_moment(centred, sample_width)
    second, third, lin_sum, proj_sum = lax.psum(
        (second_local, third_local, linear_local_part, proj_local), ("gx", "gy")
    )
    second, third = (second, third)
    covariance = second / sample_total
    skewness = third / sample_total
    linear_projection = lin_sum / total_cells
    triple_proj = proj_sum / total_cells
    factor = jnp.linalg.cholesky(covariance)
    folded = jax.scipy.linalg.cho_solve(
        (factor, True), skewness.reshape(number, number * number)
    ).reshape(number, number, number)
    growth_rate_grid = linear_term - mode_advection(folded, basis_matrix, basis_slopes, cell_width)
    perturbation_heading = (
        lax.psum(
            jnp.einsum("iyn,ayn->ia", growth_rate_grid, basis_matrix, precision=top_degree),
            ("gx", "gy"),
        )
        / total_cells
    )
    modes_tendency = growth_rate_grid - jnp.einsum(
        "yn,nbv->ybv", perturbation_heading, basis_matrix, precision=top_degree
    )
    mixed_grad = jnp.einsum("kl,ledc->kedc", covariance, basis_slopes, precision=top_degree)
    mean_rate = (
        -jnp.einsum("dc,edc->ec", mean_flat, mean_grad, precision=top_degree)
        + viscosity * mean_lap
        - jnp.einsum("kdc,kedc->ec", basis_matrix, mixed_grad, precision=top_degree)
    )
    sample_rate = sample_response(centred, linear_projection, triple_proj, covariance, sample_width)
    return (mean_rate.reshape(mean_field.shape), modes_tendency.reshape(modes.shape), sample_rate)


def solution(mesh):
    placed = (
        P(None, ("groups", "gx"), None, "gy"),
        P(None, None, ("groups", "gx"), None, "gy"),
        P(None, ("groups", "gx", "gy")),
    )
    return jax.shard_map(
        body,
        mesh=mesh,
        in_specs=placed,
        out_specs=(
            P(None, ("groups", "gx"), None, "gy"),
            P(None, None, ("groups", "gx"), None, "gy"),
            P(None, ("groups", "gx", "gy")),
        ),
        check_vma=False,
    )
```

profile of v0, /device:TPU:0, one launch (start us, length us, event | category | flops | bytes accessed | tf_op | source)
XLA Modules:
  0.0 682.1 jit_solution(13208753647194942723)
XLA Ops:
  8.2 5.1 collective-permute-start
  14.4 43.4 %psum.42 = f32[32]{0:T(128)S(1)} all-reduce(f32[32]{0:T(128)S(1)} %reduce_sum.18), channel_id=1, replica_groups=mesh['groups'=2,'gx'=4,'gy'=4] {'gx','gy'}, use_global_device_ids=true, to_apply=%region_1.2 | all-reduce | flops 32 | bytes 256 | tf_op jit(solution)/shard_map/psum | solution.py:156
  59.2 4.9 while.44
  64.1 57.6 %psum.43 = f32[32,32]{0,1:T(8,128)S(1)} all-reduce(f32[32,32]{0,1:T(8,128)S(1)} %fusion.48), channel_id=1, replica_groups=mesh['groups'=2,'gx'=4,'gy'=4] {'gx','gy'}, use_global_device_ids=true, to_apply=%region_2.3 | all-reduce | flops 1024 | bytes 8192 | tf_op jit(solution)/shard_map/psum | solution.py:162
  121.8 2.9 cholesky.16
  131.3 1.9 copy.69
  134.3 2.4 custom-call.10
  136.7 2.5 copy.75
  143.6 2.4 copy.59
  147.5 3.3 select_maximum_fusion
  153.2 2.0 copy.62
  155.2 2.0 copy.120
  158.0 4.1 copy.74
  162.1 171.2 %while.45 = (s32[]{:T(128)}, f32[32,32,32]{1,2,0:T(8,128)S(1)}, f32[8,32,3,3,128]{1,2,3,4,0:T(4,128)}, f32[8,32,3,128]{1,2,3,0:T(4,128)}, s32[]{:T(128)}, /*index=5*/s32[]{:T(128)}) while((s32[]{:T(128)}, f32[32,32,32]{1,2,0:T(8,128)S(1)}, f32[8,32,3,3,128]{1,2,3,4,0:T(4,128)}, f32[8,32,3,128]{1,2,3,0:T(4,128)}, s32[]{:T(128)}, ...), condition=%wide.region_13.14_spmd.clone, body=%wide.region_12.13_spmd.clone.sunk | while | flops 165216256 | bytes 7849043 | solution.py:64
  162.2 13.0 %convolution_bitcast_fusion.8 = f32[32,32,3,128]{0,1,2,3:T(8,128)} fusion(f32[8,32,3,3,128]{1,2,3,4,0:T(4,128)} %get-tuple-element.383, s32[]{:T(128)} %get-tuple-element.375, f32[8,32,3,128]{1,2,3,0:T(4,128)} %get-tuple-element.384), kind=kOutput, calls=%fused_computation.19.clone.1 | convolution fusion | flops 14155776 | bytes 2622464 | tf_op jit(solution)/shard_map/while/body/eval_jaxpr/rsf,nsbf->rnbf/dot_general | solution.py:55
  175.2 5.7 copy.152
  183.6 13.0 %convolution_bitcast_fusion.8 = f32[32,32,3,128]{0,1,2,3:T(8,128)} fusion(f32[8,32,3,3,128]{1,2,3,4,0:T(4,128)} %get-tuple-element.383, s32[]{:T(128)} %get-tuple-element.375, f32[8,32,3,128]{1,2,3,0:T(4,128)} %get-tuple-element.384), kind=kOutput, calls=%fused_computation.19.clone.1 | convolution fusion | flops 14155776 | bytes 2622464 | tf_op jit(solution)/shard_map/while/body/eval_jaxpr/rsf,nsbf->rnbf/dot_general | solution.py:55
  196.6 5.7 copy.152
  205.0 13.0 %convolution_bitcast_fusion.8 = f32[32,32,3,128]{0,1,2,3:T(8,128)} fusion(f32[8,32,3,3,128]{1,2,3,4,0:T(4,128)} %get-tuple-element.383, s32[]{:T(128)} %get-tuple-element.375, f32[8,32,3,128]{1,2,3,0:T(4,128)} %get-tuple-element.384), kind=kOutput, calls=%fused_computation.19.clone.1 | convolution fusion | flops 14155776 | bytes 2622464 | tf_op jit(solution)/shard_map/while/body/eval_jaxpr/rsf,nsbf->rnbf/dot_general | solution.py:55
  218.0 5.7 copy.152
  226.4 13.0 %convolution_bitcast_fusion.8 = f32[32,32,3,128]{0,1,2,3:T(8,128)} fusion(f32[8,32,3,3,128]{1,2,3,4,0:T(4,128)} %get-tuple-element.383, s32[]{:T(128)} %get-tuple-element.375, f32[8,32,3,128]{1,2,3,0:T(4,128)} %get-tuple-element.384), kind=kOutput, calls=%fused_computation.19.clone.1 | convolution fusion | flops 14155776 | bytes 2622464 | tf_op jit(solution)/shard_map/while/body/eval_jaxpr/rsf,nsbf->rnbf/dot_general | solution.py:55
  239.3 5.7 copy.152
  247.8 13.0 %convolution_bitcast_fusion.8 = f32[32,32,3,128]{0,1,2,3:T(8,128)} fusion(f32[8,32,3,3,128]{1,2,3,4,0:T(4,128)} %get-tuple-element.383, s32[]{:T(128)} %get-tuple-element.375, f32[8,32,3,128]{1,2,3,0:T(4,128)} %get-tuple-element.384), kind=kOutput, calls=%fused_computation.19.clone.1 | convolution fusion | flops 14155776 | bytes 2622464 | tf_op jit(solution)/shard_map/while/body/eval_jaxpr/rsf,nsbf->rnbf/dot_general | solution.py:55
  260.7 5.7 copy.152
  269.1 13.0 %convolution_bitcast_fusion.8 = f32[32,32,3,128]{0,1,2,3:T(8,128)} fusion(f32[8,32,3,3,128]{1,2,3,4,0:T(4,128)} %get-tuple-element.383, s32[]{:T(128)} %get-tuple-element.375, f32[8,32,3,128]{1,2,3,0:T(4,128)} %get-tuple-element.384), kind=kOutput, calls=%fused_computation.19.clone.1 | convolution fusion | flops 14155776 | bytes 2622464 | tf_op jit(solution)/shard_map/while/body/eval_jaxpr/rsf,nsbf->rnbf/dot_general | solution.py:55
  282.1 5.7 copy.152
  290.5 13.0 %convolution_bitcast_fusion.8 = f32[32,32,3,128]{0,1,2,3:T(8,128)} fusion(f32[8,32,3,3,128]{1,2,3,4,0:T(4,128)} %get-tuple-element.383, s32[]{:T(128)} %get-tuple-element.375, f32[8,32,3,128]{1,2,3,0:T(4,128)} %get-tuple-element.384), kind=kOutput, calls=%fused_computation.19.clone.1 | convolution fusion | flops 14155776 | bytes 2622464 | tf_op jit(solution)/shard_map/while/body/eval_jaxpr/rsf,nsbf->rnbf/dot_general | solution.py:55
  303.5 5.7 copy.152
  311.9 13.0 %convolution_bitcast_fusion.8 = f32[32,32,3,128]{0,1,2,3:T(8,128)} fusion(f32[8,32,3,3,128]{1,2,3,4,0:T(4,128)} %get-tuple-element.383, s32[]{:T(128)} %get-tuple-element.375, f32[8,32,3,128]{1,2,3,0:T(4,128)} %get-tuple-element.384), kind=kOutput, calls=%fused_computation.19.clone.1 | convolution fusion | flops 14155776 | bytes 2622464 | tf_op jit(solution)/shard_map/while/body/eval_jaxpr/rsf,nsbf->rnbf/dot_general | solution.py:55
  324.9 5.7 copy.152
  338.0 2.0 copy.68
  339.9 2.8 multiply_reduce_fusion
  344.8 90.8 %all-reduce.5.cloned.1.call-done = (f32[32,32,32]{2,1,0:T(8,128)}, f32[32,32,32]{2,1,0:T(8,128)}) async-done(((f32[32,32,32]{2,1,0:T(8,128)}, f32[32,32,32]{2,1,0:T(8,128)}), (f32[32,32,32]{2,1,0:T(8,128)}, f32[32,32,32]{2,1,0:T(8,128)})) %all-reduce.5.cloned.1.call-update) | async-done | bytes 262160 | tf_op jit(solution)/shard_map/psum | solution.py:162
  437.7 2.5 fusion.38
  440.5 146.9 %while.42 = (s32[]{:T(128)}, f32[8,32,3,128]{1,2,3,0:T(4,128)}, f32[8,32,3,3,128]{1,2,3,4,0:T(4,128)}, f32[8,32,3,128]{3,1,2,0:T(8,128)}, f32[32,32,32]{1,2,0:T(8,128)S(1)}, /*index=5*/s32[]{:T(128)}) while((s32[]{:T(128)}, f32[8,32,3,128]{1,2,3,0:T(4,128)}, f32[8,32,3,3,128]{1,2,3,4,0:T(4,128)}, f32[8,32,3,128]{3,1,2,0:T(8,128)}, ...), condition=%wide.region_9.10_spmd, body=%wide.region_8.9_spmd.sunk | while | flops 165150720 | bytes 12240453 | solution.py:83
  440.5 2.2 convolution_bitcast_fusion.7
  442.7 6.0 copy.151
  448.7 10.1 %fusion.90 = f32[8,32,3,128]{1,2,3,0:T(4,128)} fusion(f32[8,32,3,128]{1,2,3,0:T(4,128)} %get-tuple-element.394, s32[]{:T(128)} %get-tuple-element.393, f32[32,32,3,128]{1,0,2,3:T(8,128)} %copy.151, f32[8,32,3,3,128]{1,2,3,4,0:T(4,128)} %get-tuple-element.401), kind=kOutput, calls=%fused_computation.2.clone.1 | convolution fusion | flops 14155776 | bytes 7341056 | tf_op jit(solution)/shard_map/while/body/eval_jaxpr/nyfu,ytfu->ntu/dot_general | solution.py:80
  458.8 2.2 convolution_bitcast_fusion.7
  461.0 6.0 copy.151
  467.0 10.1 %fusion.90 = f32[8,32,3,128]{1,2,3,0:T(4,128)} fusion(f32[8,32,3,128]{1,2,3,0:T(4,128)} %get-tuple-element.394, s32[]{:T(128)} %get-tuple-element.393, f32[32,32,3,128]{1,0,2,3:T(8,128)} %copy.151, f32[8,32,3,3,128]{1,2,3,4,0:T(4,128)} %get-tuple-element.401), kind=kOutput, calls=%fused_computation.2.clone.1 | convolution fusion | flops 14155776 | bytes 7341056 | tf_op jit(solution)/shard_map/while/body/eval_jaxpr/nyfu,ytfu->ntu/dot_general | solution.py:80
  477.2 2.2 convolution_bitcast_fusion.7
  479.3 6.0 copy.151
  485.4 10.2 %fusion.90 = f32[8,32,3,128]{1,2,3,0:T(4,128)} fusion(f32[8,32,3,128]{1,2,3,0:T(4,128)} %get-tuple-element.394, s32[]{:T(128)} %get-tuple-element.393, f32[32,32,3,128]{1,0,2,3:T(8,128)} %copy.151, f32[8,32,3,3,128]{1,2,3,4,0:T(4,128)} %get-tuple-element.401), kind=kOutput, calls=%fused_computation.2.clone.1 | convolution fusion | flops 14155776 | bytes 7341056 | tf_op jit(solution)/shard_map/while/body/eval_jaxpr/nyfu,ytfu->ntu/dot_general | solution.py:80
  495.5 2.2 convolution_bitcast_fusion.7
  497.7 6.0 copy.151
  503.7 10.2 %fusion.90 = f32[8,32,3,128]{1,2,3,0:T(4,128)} fusion(f32[8,32,3,128]{1,2,3,0:T(4,128)} %get-tuple-element.394, s32[]{:T(128)} %get-tuple-element.393, f32[32,32,3,128]{1,0,2,3:T(8,128)} %copy.151, f32[8,32,3,3,128]{1,2,3,4,0:T(4,128)} %get-tuple-element.401), kind=kOutput, calls=%fused_computation.2.clone.1 | convolution fusion | flops 14155776 | bytes 7341056 | tf_op jit(solution)/shard_map/while/body/eval_jaxpr/nyfu,ytfu->ntu/dot_general | solution.py:80
  513.8 2.2 convolution_bitcast_fusion.7
  516.0 6.0 copy.151
  522.0 10.2 %fusion.90 = f32[8,32,3,128]{1,2,3,0:T(4,128)} fusion(f32[8,32,3,128]{1,2,3,0:T(4,128)} %get-tuple-element.394, s32[]{:T(128)} %get-tuple-element.393, f32[32,32,3,128]{1,0,2,3:T(8,128)} %copy.151, f32[8,32,3,3,128]{1,2,3,4,0:T(4,128)} %get-tuple-element.401), kind=kOutput, calls=%fused_computation.2.clone.1 | convolution fusion | flops 14155776 | bytes 7341056 | tf_op jit(solution)/shard_map/while/body/eval_jaxpr/nyfu,ytfu->ntu/dot_general | solution.py:80
  532.2 2.2 convolution_bitcast_fusion.7
  534.4 6.0 copy.151
  540.4 10.2 %fusion.90 = f32[8,32,3,128]{1,2,3,0:T(4,128)} fusion(f32[8,32,3,128]{1,2,3,0:T(4,128)} %get-tuple-element.394, s32[]{:T(128)} %get-tuple-element.393, f32[32,32,3,128]{1,0,2,3:T(8,128)} %copy.151, f32[8,32,3,3,128]{1,2,3,4,0:T(4,128)} %get-tuple-element.401), kind=kOutput, calls=%fused_computation.2.clone.1 | convolution fusion | flops 14155776 | bytes 7341056 | tf_op jit(solution)/shard_map/while/body/eval_jaxpr/nyfu,ytfu->ntu/dot_general | solution.py:80
  550.5 2.2 convolution_bitcast_fusion.7
  552.7 6.0 copy.151
  558.7 10.2 %fusion.90 = f32[8,32,3,128]{1,2,3,0:T(4,128)} fusion(f32[8,32,3,128]{1,2,3,0:T(4,128)} %get-tuple-element.394, s32[]{:T(128)} %get-tuple-element.393, f32[32,32,3,128]{1,0,2,3:T(8,128)} %copy.151, f32[8,32,3,3,128]{1,2,3,4,0:T(4,128)} %get-tuple-element.401), kind=kOutput, calls=%fused_computation.2.clone.1 | convolution fusion | flops 14155776 | bytes 7341056 | tf_op jit(solution)/shard_map/while/body/eval_jaxpr/nyfu,ytfu->ntu/dot_general | solution.py:80
  568.9 2.2 convolution_bitcast_fusion.7
  571.0 6.0 copy.151
  577.1 10.2 %fusion.90 = f32[8,32,3,128]{1,2,3,0:T(4,128)} fusion(f32[8,32,3,128]{1,2,3,0:T(4,128)} %get-tuple-element.394, s32[]{:T(128)} %get-tuple-element.393, f32[32,32,3,128]{1,0,2,3:T(8,128)} %copy.151, f32[8,32,3,3,128]{1,2,3,4,0:T(4,128)} %get-tuple-element.401), kind=kOutput, calls=%fused_computation.2.clone.1 | convolution fusion | flops 14155776 | bytes 7341056 | tf_op jit(solution)/shard_map/while/body/eval_jaxpr/nyfu,ytfu->ntu/dot_general | solution.py:80
  587.4 11.1 %bitcast_subtract_fusion = (f32[32,3,1024]{0,1,2:T(4,128)S(1)}, f32[32,3,1024]{0,1,2:T(4,128)S(1)}) fusion(f32[8,32,3,128]{1,2,3,0:T(4,128)} %get-tuple-element.102, f32[32,3,1,8,128]{0,1,4,3,2:T(4,128)} %copy.68, f32[3,3,1024]{1,0,2:T(4,128)} %bitcast.239, f32[32,3,1024]{0,1,2:T(4,128)} %copy.67, f32[1024,32,3]{1,2,0:T(4,128)} %copy.134), kind=kOutput, calls=%fused_computation.37 | convolution fusion | flops 3833856 | bytes 2396160 | tf_op jit(solution)/shard_map/kdc,edc->kec/dot_general | solution.py:147
  600.6 59.0 %all-reduce.1 = (f32[32,32]{0,1:T(8,128)S(1)}, f32[32,32]{0,1:T(8,128)S(1)}) all-reduce(f32[32,32]{0,1:T(8,128)S(1)} %fusion.25, f32[32,32]{0,1:T(8,128)S(1)} %fusion.28), channel_id=1, replica_groups=mesh['groups'=2,'gx'=4,'gy'=4] {'gx','gy'}, use_global_device_ids=true, to_apply=%region_10.11 | all-reduce | flops 2048 | bytes 16384 | tf_op jit(solution)/shard_map/psum | solution.py:176
  661.4 4.2 while.43
  668.5 3.5 sub.45
  672.0 2.8 copy.89
  (136 shorter events, 65.9 us)
Async XLA Ops:
  7.2 428.4 %all-reduce.5.cloned.1.call-start = ((), (), s32[]{:S(2)}) async-start(), calls=%async_computation | async-start | bytes 2097152 | tf_op jit(solution)/shard_map/psum | solution.py:162
  8.2 117.2 %collective-permute-start = (f32[33,3,1,8,128]{4,3,1,0,2:T(8,128)S(1)}, f32[33,3,1,8,128]{4,3,1,0,2:T(8,128)S(1)}, u32[]{:S(2)}, u32[]{:S(2)}) collective-permute-start(f32[33,3,1,8,128]{4,3,1,0,2:T(8,128)S(1)} %pad_maximum_fusion.11), channel_id=1, source_target_pairs={{4,0},{8,4},{12,8},{0,12},{5,1},{9,5},{13,9},{1,13},{6,2},{10,6},{... | collective-permute-start | bytes 1216520 | tf_op jit(solution)/shard_map/ppermute | solution.py:21
  13.3 112.1 %collective-permute-start.1 = (f32[33,3,1,8,128]{4,3,1,0,2:T(8,128)S(1)}, f32[33,3,1,8,128]{4,3,1,0,2:T(8,128)S(1)}, u32[]{:S(2)}, u32[]{:S(2)}) collective-permute-start(f32[33,3,1,8,128]{4,3,1,0,2:T(8,128)S(1)} %pad_maximum_fusion.11), channel_id=1, source_target_pairs={{0,4},{4,8},{8,12},{12,0},{1,5},{5,9},{9,13},{13,1},{2,6},{6,10},{... | collective-permute-start | bytes 1216520 | tf_op jit(solution)/shard_map/ppermute | solution.py:19
  59.2 66.3 %copy-start = (f32[32,3,1,8,128]{4,3,2,1,0:T(8,128)S(1)}, f32[32,3,1,8,128]{4,3,2,1,0:T(8,128)}, u32[]{:S(2)}) copy-start(f32[32,3,1,8,128]{4,3,2,1,0:T(8,128)} %param.12) | copy-start | bytes 1179652
  59.2 66.3 %copy-start.5 = (f32[3,1,8,128]{3,2,1,0:T(8,128)S(1)}, f32[3,1,8,128]{3,2,1,0:T(8,128)}, u32[]{:S(2)}) copy-start(f32[3,1,8,128]{3,2,1,0:T(8,128)} %param.11) | copy-start | bytes 36868
  128.8 13.3 %collective-permute-start.2 = (f32[33,3,3,8,1]{0,3,4,2,1:T(8,128)S(1)}, f32[33,3,3,8,1]{0,3,4,2,1:T(8,128)}, u32[]{:S(2)}, u32[]{:S(2)}) collective-permute-start(f32[33,3,3,8,1]{0,3,4,2,1:T(8,128)S(1)} %copy.56), channel_id=1, source_target_pairs={{1,0},{2,1},{3,2},{0,3},{5,4},{6,5},{7,6},{4,7},{9,8},{10,9},{11,1... | collective-permute-start | bytes 28520 | tf_op jit(solution)/shard_map/ppermute | solution.py:21
  130.1 13.5 %collective-permute-start.3 = (f32[33,3,3,8,1]{0,3,4,2,1:T(8,128)}, f32[33,3,3,8,1]{0,3,4,2,1:T(8,128)}, u32[]{:S(2)}, u32[]{:S(2)}) collective-permute-start(f32[33,3,3,8,1]{0,3,4,2,1:T(8,128)} %copy.58), channel_id=1, source_target_pairs={{0,1},{1,2},{2,3},{3,0},{4,5},{5,6},{6,7},{7,4},{8,9},{9,10},{10,1... | collective-permute-start | bytes 28520 | tf_op jit(solution)/shard_map/ppermute | solution.py:19
  146.0 1.5 copy-start.1
  153.2 4.0 copy-start.3
  335.8 2.1 copy-start.4
  336.0 3.9 copy-start.2
  599.6 61.7 %copy-start.6 = (f32[4,32,256]{2,1,0:T(8,128)S(1)}, f32[4,32,256]{2,1,0:T(8,128)}, u32[]{:S(2)}) copy-start(f32[4,32,256]{2,1,0:T(8,128)} %custom-call.14) | copy-start | bytes 393220
Sparse Core Ops, SparseCore 0:
  344.3 91.2 all-reduce.4
where the time goes:
time: 691 us; the launch traced here: 682 us
  matrix products  241 us (35%)
  blocking collectives  160 us (23%)
  local copies, waits for them, and re-layouts  141 us (20%)
  waiting for transfers between devices  90.9 us (13%)
  other arithmetic  27.6 us (4%)
  between operations  14.9 us (2%)
    dot_general x8, matrix products, triple_step_forward(): jnp.einsum('rsf,nsbf->rnbf', value_entries, slope_arrays, precision=top_d...  104 us
    psum x1, waiting for transfers between devices, body(): lax.psum((second_local, third_local, linear_local_part, proj_local), ('gx...  90.8 us
    dot_general x8, matrix products, mode_step_forward(): jnp.einsum('nyfu,ytfu->ntu', velocity_field, slope_arrays, precision=top_...  81.2 us
    psum x1, blocking collectives, body(): lax.psum(jnp.einsum('iyn,ayn->ia', growth_rate_grid, basis_matrix, precis...  59 us
    psum x1, blocking collectives, body(): lax.psum((second_local, third_local, linear_local_part, proj_local), ('gx...  57.6 us
    dot_general x8, local copies, waits for them, and re-layouts, mode_step_forward(): jnp.einsum('ikl,kdc->ildc', folded, value_entries, precision=top_degree)  48.1 us
    transpose x8, local copies, waits for them, and re-layouts, triple_step_forward(): jnp.einsum('rsf,nsbf->rnbf', value_entries, slope_arrays, precision=top_d...  45.8 us
    psum x1, blocking collectives, body(): average = lax.psum(jnp.sum(samples, axis=1), ('gx', 'gy')) / sample_total  43.4 us
  transfers between devices with their start and end apart: 5, of which 1 were waited for; matrix products, arithmetic and copies ran while one was open for 4% of the time, Pallas kernels for 0%

commit v1 on v0

v1 whole, which is shorter than its diff:
```python
import functools

import jax
import jax.numpy as jnp
from jax import lax
from jax.experimental import pallas as pl
from jax.experimental.pallas import tpu as pltpu
from jax.sharding import PartitionSpec as P

MESH = pl.DeviceIdType.MESH
top_degree = lax.Precision.HIGHEST
viscosity = 0.2
f32, bf16 = jnp.float32, jnp.bfloat16

K = 32
HALF = 16
NZ = 8
LANES = 128
CELLS = NZ * LANES
PAIRS = HALF * HALF + HALF * K
WIDE = PAIRS + LANES
ROWS = 40


def split(x):
    hi = x.astype(bf16)
    return hi, (x - hi.astype(f32)).astype(bf16)


def dot(a, b, precision=None):
    return lax.dot_general(
        a, b, (((1,), (0,)), ((), ())), precision=precision, preferred_element_type=f32
    )


def dot_nt(a, b, precision=None):
    return lax.dot_general(
        a, b, (((1,), (1,)), ((), ())), precision=precision, preferred_element_type=f32
    )


def inverse(matrix):
    lane = lax.broadcasted_iota(jnp.int32, (K, LANES), 1)
    row = lax.broadcasted_iota(jnp.int32, (K, LANES), 0)
    m = jnp.where(lane < K, matrix, jnp.where(lane == row + K, 1.0, 0.0))
    for k in range(K):
        pivot_row = m[k : k + 1, :] / m[k : k + 1, k : k + 1]
        m = jnp.where(row == k, pivot_row, m - m[:, k : k + 1] * pivot_row)
    return m[:, K : 2 * K]


def kernel(
    gx,
    gy,
    mean_ref,
    modes_ref,
    samples_ref,
    mean_out,
    modes_out,
    samples_out,
    xm,
    xp,
    f,
    g,
    lap,
    lin,
    mt,
    bh,
    bl,
    ph,
    plo,
    centred,
    coef,
    avg_own,
    avg_y,
    avg_mid,
    avg_x,
    edge_send,
    edge_recv,
    sb,
    sr1,
    s1,
    sr2,
    sfull,
    tb,
    tr1,
    t1,
    tr2,
    tfull,
    halo_send,
    halo_recv,
    edge_ss,
    edge_rs,
    ay_ss,
    ay_rs,
    ax_ss,
    ax_rs,
    s_ss,
    s_rs,
    sx_ss,
    sx_rs,
    sg_ss,
    sg_rs,
    t_ss,
    t_rs,
    tx_ss,
    tx_rs,
    tg_ss,
    tg_rs,
):
    ix, iy = lax.axis_index("gx"), lax.axis_index("gy")
    members = gx * gy
    sample_total = samples_ref.shape[1] * members
    total_cells = CELLS * members

    barrier = pltpu.get_barrier_semaphore()
    for off in range(1, gx):
        pl.semaphore_signal(
            barrier, inc=1, device_id={"gx": lax.rem(ix + off, gx)}, device_id_type=MESH
        )
    for off in range(1, gy):
        pl.semaphore_signal(
            barrier, inc=1, device_id={"gy": lax.rem(iy + off, gy)}, device_id_type=MESH
        )
    pl.semaphore_wait(barrier, gx + gy - 2)

    def send(src, dst, ss, rs, axis, target):
        copy = pltpu.make_async_remote_copy(
            src_ref=src,
            dst_ref=dst,
            send_sem=ss,
            recv_sem=rs,
            device_id={axis: target},
            device_id_type=MESH,
        )
        copy.start()
        return copy

    x_next, x_prev = lax.rem(ix + 1, gx), lax.rem(ix + gx - 1, gx)
    y_next, y_prev = lax.rem(iy + 1, gy), lax.rem(iy + gy - 1, gy)

    part = samples_ref[:, 0:LANES]
    for z in range(1, samples_ref.shape[1] // LANES):
        part = part + samples_ref[:, z * LANES : (z + 1) * LANES]
    avg_own[...] = part

    def spread(src, slots, ss, rs, axis, index, count):
        return [
            send(src, slots.at[off], ss.at[off], rs.at[off], axis, lax.rem(index + off, count))
            for off in range(1, count)
        ]

    avg_copies = spread(avg_own, avg_y, ay_ss, ay_rs, "gy", iy, gy)

    halo = []
    halo.append(send(mean_ref, xm.at[768:792], halo_send.at[0], halo_recv.at[0], "gx", x_next))
    halo.append(send(mean_ref, xp.at[768:792], halo_send.at[1], halo_recv.at[1], "gx", x_prev))
    for c in range(2):
        rows = slice(c * 384, (c + 1) * 384)
        s = 2 + 2 * c
        halo.append(
            send(modes_ref.at[rows], xm.at[rows], halo_send.at[s], halo_recv.at[s], "gx", x_next)
        )
        halo.append(
            send(
                modes_ref.at[rows],
                xp.at[rows],
                halo_send.at[s + 1],
                halo_recv.at[s + 1],
                "gx",
                x_prev,
            )
        )

    lane = lax.broadcasted_iota(jnp.int32, (ROWS, LANES), 1)
    to_next = jnp.zeros((ROWS, LANES), f32)
    to_prev = jnp.zeros((ROWS, LANES), f32)
    for e in range(3):
        for z in range(NZ):
            j = e * NZ + z
            cols = slice(z * LANES, (z + 1) * LANES)
            f[e, 0:K, cols] = modes_ref[pl.ds(j, K, stride=24), :]
            f[e, K:ROWS, cols] = jnp.broadcast_to(mean_ref[j : j + 1, :], (ROWS - K, LANES))
            piece = f[e, :, cols]
            to_next = jnp.where(lane == j, pltpu.roll(piece, j + 1, 1), to_next)
            to_prev = jnp.where(lane == j, pltpu.roll(piece, j, 1) if j else piece, to_prev)
    edge_send[0] = to_next
    edge_send[1] = to_prev
    edges = [
        send(edge_send.at[0], edge_recv.at[0], edge_ss.at[0], edge_rs.at[0], "gy", y_next),
        send(edge_send.at[1], edge_recv.at[1], edge_ss.at[1], edge_rs.at[1], "gy", y_prev),
    ]
    for e in range(3):
        hi, lo = split(f[e, 0:K, :])
        mt[e, 0:K, :] = hi
        mt[e, K : 2 * K, :] = lo

    for copy in avg_copies:
        copy.wait()
    total = avg_own[...]
    for off in range(1, gy):
        total = total + avg_y[off]
    avg_mid[...] = total
    avg_copies = spread(avg_mid, avg_x, ax_ss, ax_rs, "gx", ix, gx)

    for copy in edges:
        copy.wait()
    for e in range(3):
        for z in range(NZ):
            j = e * NZ + z
            cols = slice(z * LANES, (z + 1) * LANES)
            piece = f[e, :, cols]
            before = jnp.where(
                lane == 0, pltpu.roll(edge_recv[0], LANES - j, 1) if j else edge_recv[0],
                pltpu.roll(piece, 1, 1),
            )
            after = jnp.where(
                lane == LANES - 1, pltpu.roll(edge_recv[1], LANES - 1 - j, 1),
                pltpu.roll(piece, LANES - 1, 1),
            )
            zero = jnp.zeros_like(piece)
            below = f[e, :, (z - 1) * LANES : z * LANES] if z else zero
            above = f[e, :, (z + 1) * LANES : (z + 2) * LANES] if z < NZ - 1 else zero
            g[1, e, :, cols] = (after - before) * 0.5
            g[2, e, :, cols] = (above - below) * 0.5
            lap[e, :, cols] = after + before + above + below - 6.0 * piece

    for copy in avg_copies:
        copy.wait()
    total = avg_mid[...]
    for off in range(1, gx):
        total = total + avg_x[off]
    average = jnp.sum(total, axis=1, keepdims=True) / sample_total
    centred[...] = samples_ref[...] - average

    def pair_low(l, _):
        row = pl.ds(pl.multiple_of(l * HALF, HALF), HALF)
        hi, lo = split(centred[0:HALF, :] * centred[pl.ds(l, 1), :])
        ph[row, :] = hi
        plo[row, :] = lo
        return 0

    def pair_high(l, _):
        row = pl.ds(pl.multiple_of(HALF * HALF + l * K, HALF), K)
        hi, lo = split(centred[...] * centred[pl.ds(l + HALF, 1), :])
        ph[row, :] = hi
        plo[row, :] = lo
        return 0

    lax.fori_loop(0, HALF, pair_low, 0)
    lax.fori_loop(0, HALF, pair_high, 0)
    c_hi, c_lo = split(centred[...])
    c_both = jnp.concatenate([c_hi, c_lo], axis=0)
    for r in range(PAIRS // 256):
        rows = slice(r * 256, (r + 1) * 256)
        first = dot_nt(c_both, ph[rows, :])
        sb[:, rows] = first[0:K] + first[K : 2 * K] + dot_nt(c_hi, plo[rows, :])
    sb[:, PAIRS:WIDE] = jnp.zeros((K, LANES), f32)
    sb[:, PAIRS : PAIRS + K] = dot_nt(centred[...], centred[...], top_degree)

    own_rows = pl.ds(pl.multiple_of(iy * 8, 8), 8)

    def scatter(src, slots, ss, rs):
        copies = []
        for off in range(1, gy):
            target = lax.rem(iy + off, gy)
            rows = pl.ds(pl.multiple_of(target * 8, 8), 8)
            copies.append(send(src.at[rows], slots.at[off], ss.at[off], rs.at[off], "gy", target))
        return copies

    def gather(full, ss, rs):
        return [
            send(
                full.at[own_rows],
                full.at[own_rows],
                ss.at[off],
                rs.at[off],
                "gy",
                lax.rem(iy + off, gy),
            )
            for off in range(1, gy)
        ]

    def finish_scatter(copies, src, slots, out):
        for copy in copies:
            copy.wait()
        summed = src[own_rows, :]
        for off in range(1, gy):
            summed = summed + slots[off]
        out[...] = summed

    def finish_spread(copies, own, slots, full):
        for copy in copies:
            copy.wait()
        summed = own[...]
        for off in range(1, gx):
            summed = summed + slots[off]
        full[own_rows, :] = summed

    copies = scatter(sb, sr1, s_ss, s_rs)
    finish_scatter(copies, sb, sr1, s1)
    copies = spread(s1, sr2, sx_ss, sx_rs, "gx", ix, gx)
    finish_spread(copies, s1, sr2, sfull)
    copies = gather(sfull, sg_ss, sg_rs)
    for copy in copies:
        copy.wait()

    second = sfull[:, PAIRS:WIDE]
    inv = inverse(second)
    folded = dot(inv, sfull[:, 0:PAIRS], top_degree)
    p_k = lax.broadcasted_iota(jnp.int32, (K, PAIRS), 1)
    low = p_k < HALF * HALF
    q = p_k - HALF * HALF
    k_of = jnp.where(low, p_k & (HALF - 1), q & (K - 1))
    l_of = jnp.where(low, p_k >> 4, HALF + (q >> 5))
    row_of = lax.broadcasted_iota(jnp.int32, (K, PAIRS), 0)
    choose = jnp.where(k_of == row_of, 1.0, 0.0).astype(f32)
    spread_cov = dot(second[:, 0:K] / sample_total, choose, top_degree)
    cov_row = jnp.sum(jnp.where(l_of == row_of, spread_cov, 0.0), axis=0, keepdims=True)
    full_coef = jnp.concatenate([folded, jnp.broadcast_to(cov_row, (HALF, PAIRS))], axis=0)
    hi, lo = split(full_coef)
    coef[0:48, :] = hi
    coef[48:96, :] = lo

    for copy in halo:
        copy.wait()
    for e in range(3):
        for z in range(NZ):
            j = e * NZ + z
            cols = slice(z * LANES, (z + 1) * LANES)
            before = xm[pl.ds(j, K, stride=24), :]
            after = xp[pl.ds(j, K, stride=24), :]
            g[0, e, 0:K, cols] = (after - before) * 0.5
            lap[e, 0:K, cols] = lap[e, 0:K, cols] + (after + before)
            before = xm[768 + j : 769 + j, :]
            after = xp[768 + j : 769 + j, :]
            g[0, e, K:ROWS, cols] = jnp.broadcast_to((after - before) * 0.5, (ROWS - K, LANES))
            lap[e, K:ROWS, cols] = lap[e, K:ROWS, cols] + (after + before)

    def advect_low(l, _):
        row = pl.ds(pl.multiple_of(l * HALF, HALF), HALF)
        for e in range(3):
            value = f[0, 0:HALF, :] * g[0, e, pl.ds(l, 1), :]
            for d in range(1, 3):
                value = value + f[d, 0:HALF, :] * g[d, e, pl.ds(l, 1), :]
            hi, lo = split(value)
            bh[e, row, :] = hi
            bl[e, row, :] = lo
        return 0

    def advect_high(i, _):
        l = i + HALF
        base = pl.multiple_of(HALF * HALF + i * K, K)
        row = pl.ds(base, HALF)
        diag = pl.ds(pl.multiple_of(base + HALF, HALF), HALF)
        for e in range(3):
            value = f[0, 0:HALF, :] * g[0, e, pl.ds(l, 1), :]
            value = value + g[0, e, 0:HALF, :] * f[0, pl.ds(l, 1), :]
            other = f[0, HALF:K, :] * g[0, e, pl.ds(l, 1), :]
            for d in range(1, 3):
                value = value + f[d, 0:HALF, :] * g[d, e, pl.ds(l, 1), :]
                value = value + g[d, e, 0:HALF, :] * f[d, pl.ds(l, 1), :]
                other = other + f[d, HALF:K, :] * g[d, e, pl.ds(l, 1), :]
            hi, lo = split(value)
            bh[e, row, :] = hi
            bl[e, row, :] = lo
            hi, lo = split(other)
            bh[e, diag, :] = hi
            bl[e, diag, :] = lo
        return 0

    lax.fori_loop(0, HALF, advect_low, 0)
    lax.fori_loop(0, HALF, advect_high, 0)

    for e in range(3):
        forced = f[0, K : K + 1, :] * g[0, e] + f[0] * g[0, e, K : K + 1, :]
        for d in range(1, 3):
            forced = forced + f[d, K : K + 1, :] * g[d, e] + f[d] * g[d, e, K : K + 1, :]
        lin[e, 0:K] = viscosity * lap[e, 0:K] - forced[0:K]
        lin[e, K:ROWS] = viscosity * lap[e, K:ROWS] - 0.5 * forced[K:ROWS]

    for r in range(PAIRS // 256):
        rows = slice(r * 256, (r + 1) * 256)
        value = jnp.zeros((K, 256), f32)
        for e in range(3):
            first = dot_nt(mt[e], bh[e, rows, :])
            value = value + (first[0:K] + first[K : 2 * K] + dot_nt(mt[e, 0:K], bl[e, rows, :]))
        tb[:, rows] = value
    lin_t = jnp.zeros((K, K), f32)
    lin_n = jnp.zeros((K, K), f32)
    for e in range(3):
        lin_hi, lin_lo = split(lin[e, 0:K, :])
        m_hi, m_lo = mt[e, 0:K], mt[e, K : 2 * K]
        lin_t = lin_t + (dot_nt(m_hi, lin_hi) + dot_nt(m_lo, lin_hi) + dot_nt(m_hi, lin_lo))
        lin_n = lin_n + (dot_nt(lin_hi, m_hi) + dot_nt(lin_hi, m_lo) + dot_nt(lin_lo, m_hi))
    tb[:, PAIRS:WIDE] = jnp.zeros((K, LANES), f32)
    tb[:, PAIRS : PAIRS + K] = lin_t
    tb[:, PAIRS + K : PAIRS + 2 * K] = lin_n

    def tendency(e):
        def step(i, _):
            cols = pl.ds(pl.multiple_of(i * 256, 256), 256)
            first = dot(coef[...], bh[e, :, cols])
            value = first[0:ROWS] + first[48 : 48 + ROWS] + dot(coef[0:48], bl[e, :, cols])[0:ROWS]
            lin[e, :, cols] = lin[e, :, cols] - value
            return 0

        lax.fori_loop(0, CELLS // 256, step, 0)

    copies = scatter(tb, tr1, t_ss, t_rs)
    tendency(0)
    finish_scatter(copies, tb, tr1, t1)
    copies = spread(t1, tr2, tx_ss, tx_rs, "gx", ix, gx)
    tendency(1)
    finish_spread(copies, t1, tr2, tfull)
    copies = gather(tfull, tg_ss, tg_rs)
    tendency(2)
    for e in range(3):
        for z in range(NZ):
            j = e * NZ + z
            mean_out[j : j + 1, :] = lin[e, K : K + 1, z * LANES : (z + 1) * LANES]
    for copy in copies:
        copy.wait()

    triple = tfull[:, 0:PAIRS] / total_cells
    ends = tfull[:, PAIRS:WIDE] / total_cells
    tangent = ends[:, K : 2 * K] - dot_nt(full_coef[0:K], triple, top_degree)
    a_hi, a_lo = split(tangent)
    a_both = jnp.concatenate([a_hi, a_lo], axis=0)
    for e in range(3):
        first = dot(a_both, mt[e, 0:K])
        value = first[0:K] + first[K : 2 * K] + dot(a_hi, mt[e, K : 2 * K])
        value = lin[e, 0:K, :] - value
        for z in range(NZ):
            modes_out[pl.ds(e * NZ + z, K, stride=24), :] = value[:, z * LANES : (z + 1) * LANES]

    offset = jnp.sum(triple * cov_row, axis=1, keepdims=True)
    hi, lo = split(triple)
    t_both = jnp.concatenate([hi, lo], axis=0)
    l_hi, l_lo = split(ends[:, 0:K])
    l_both = jnp.concatenate([l_hi, l_lo], axis=0)
    for i in range(samples_ref.shape[1] // 256):
        cols = slice(i * 256, (i + 1) * 256)
        first = dot(t_both, ph[:, cols])
        value = first[0:K] + first[K : 2 * K] + dot(hi, plo[:, cols])
        s_hi, s_lo = split(centred[:, cols])
        first = dot(l_both, s_hi)
        direct = first[0:K] + first[K : 2 * K] + dot(l_hi, s_lo)
        samples_out[:, cols] = direct - value + offset


def body(mean_field, modes, samples):
    gx, gy = lax.axis_size("gx"), lax.axis_size("gy")
    vmem = pl.BlockSpec(memory_space=pltpu.VMEM)
    count = samples.shape[1]
    dma = lambda n: pltpu.SemaphoreType.DMA((n,))
    scratch = [
        pltpu.VMEM((792, LANES), f32),
        pltpu.VMEM((792, LANES), f32),
        pltpu.VMEM((3, ROWS, CELLS), f32),
        pltpu.VMEM((3, 3, ROWS, CELLS), f32),
        pltpu.VMEM((3, ROWS, CELLS), f32),
        pltpu.VMEM((3, ROWS, CELLS), f32),
        pltpu.VMEM((3, 2 * K, CELLS), bf16),
        pltpu.VMEM((3, PAIRS, CELLS), bf16),
        pltpu.VMEM((3, PAIRS, CELLS), bf16),
        pltpu.VMEM((PAIRS, count), bf16),
        pltpu.VMEM((PAIRS, count), bf16),
        pltpu.VMEM((K, count), f32),
        pltpu.VMEM((96, PAIRS), bf16),
        pltpu.VMEM((K, LANES), f32),
        pltpu.VMEM((gy, K, LANES), f32),
        pltpu.VMEM((K, LANES), f32),
        pltpu.VMEM((gx, K, LANES), f32),
        pltpu.VMEM((2, ROWS, LANES), f32),
        pltpu.VMEM((2, ROWS, LANES), f32),
    ]
    for _ in range(2):
        scratch += [
            pltpu.VMEM((K, WIDE), f32),
            pltpu.VMEM((gy, 8, WIDE), f32),
            pltpu.VMEM((8, WIDE), f32),
            pltpu.VMEM((gx, 8, WIDE), f32),
            pltpu.VMEM((K, WIDE), f32),
        ]
    sems = [dma(6), dma(6), dma(2), dma(2), dma(gy), dma(gy), dma(gx), dma(gx)]
    for _ in range(2):
        sems += [dma(gy), dma(gy), dma(gx), dma(gx), dma(gy), dma(gy)]
    mean_rate, modes_rate, sample_rate = pl.pallas_call(
        functools.partial(kernel, gx, gy),
        out_shape=(
            jax.ShapeDtypeStruct((3 * NZ, LANES), f32),
            jax.ShapeDtypeStruct((K * 3 * NZ, LANES), f32),
            jax.ShapeDtypeStruct(samples.shape, f32),
        ),
        in_specs=[vmem] * 3,
        out_specs=(vmem,) * 3,
        scratch_shapes=scratch + sems,
        compiler_params=pltpu.CompilerParams(
            collective_id=0, has_side_effects=True, vmem_limit_bytes=48 * 1024 * 1024
        ),
    )(mean_field.reshape(3 * NZ, LANES), modes.reshape(K * 3 * NZ, LANES), samples)
    return (mean_rate.reshape(mean_field.shape), modes_rate.reshape(modes.shape), sample_rate)


def solution(mesh):
    placed = (
        P(None, ("groups", "gx"), None, "gy"),
        P(None, None, ("groups", "gx"), None, "gy"),
        P(None, ("groups", "gx", "gy")),
    )
    return jax.shard_map(body, mesh=mesh, in_specs=placed, out_specs=placed, check_vma=False)
```

time: 691 us -> 67.4 us (0.10); the launches traced: 682 us -> 67.1 us
  matrix products: 241 us -> 0 us
  blocking collectives: 160 us -> 0 us
  local copies, waits for them, and re-layouts: 141 us -> 4.6 us
  waiting for transfers between devices: 90.9 us -> 0 us
  Pallas kernels: 0 us -> 61.9 us
  other arithmetic: 27.6 us -> 0 us
  between operations: 14.9 us -> 0.65 us
    dot_general x50 -> x0, matrix products: 238 us -> none  [the longest x8 104 us: triple_step_forward(): jnp.einsum('rsf,nsbf->rnbf', value_entries, slope_arrays, precision=top_d...]
    psum x3 -> x0, blocking collectives: 160 us -> none  [the longest x1 59 us: body(): lax.psum(jnp.einsum('iyn,ayn->ia', growth_rate_grid, basis_matrix, precis...]
    psum x1 -> x0, waiting for transfers between devices: 90.8 us -> none  [body(): lax.psum((second_local, third_local, linear_local_part, proj_local), ('gx...]
    pallas_call x0 -> x1, Pallas kernels: none -> 61.9 us  [body(): pl.pallas_call(functools.partial(kernel, gx, gy), out_shape=(jax.ShapeDty...]
    dot_general x9 -> x0, local copies, waits for them, and re-layouts: 49.9 us -> none  [the longest x8 48.1 us: mode_step_forward(): jnp.einsum('ikl,kdc->ildc', folded, value_entries, precision=top_degree)]
    transpose x8 -> x0, local copies, waits for them, and re-layouts: 45.8 us -> none  [triple_step_forward(): jnp.einsum('rsf,nsbf->rnbf', value_entries, slope_arrays, precision=top_d...]
    another operation x8 -> x0, other arithmetic: 10.4 us -> none  [the longest x3 3.72 us: derivatives(): jnp.stack([(x_plus - x_minus) * 0.5, (y_plus - y_minus) * 0.5, (z_plus -...]
    squeeze x24 -> x0, local copies, waits for them, and re-layouts: 8.84 us -> none  [the longest x16 8.77 us: triple_products(): lax.scan(triple_step_forward, jnp.zeros((number, number, number), jnp.flo...]
  transfers between devices with their start and end apart: 5 -> 0, of which waited for: 1 -> 0; matrix products, arithmetic and copies ran while one was open for 4% -> 0% of each run, Pallas kernels for 0% -> 0%
where the time goes in v1:
time: 67.4 us; the launch traced here: 67.1 us
  Pallas kernels  61.9 us (92%)
  local copies, waits for them, and re-layouts  4.6 us (7%)
    pallas_call x1, Pallas kernels, body(): pl.pallas_call(functools.partial(kernel, gx, gy), out_shape=(jax.ShapeDty...  61.9 us
    unnamed x9, local copies, waits for them, and re-layouts  4.6 us

profile of v1, /device:TPU:0, one launch (start us, length us, event | category | flops | bytes accessed | tf_op | source)
XLA Modules:
  0.0 67.1 jit_solution(12363451246943650211)
XLA Ops:
  0.6 0.0 copy-start
  0.6 1.0 %copy-done = f32[32,3,1,8,128]{4,3,2,1,0:T(8,128)S(1)} copy-done((f32[32,3,1,8,128]{4,3,2,1,0:T(8,128)S(1)}, f32[32,3,1,8,128]{4,3,2,1,0:T(8,128)}, u32[]{:S(2)}) %copy-start) | copy-done | bytes 393240
  1.6 0.0 copy-start.1
  1.6 0.9 %copy-done.1 = f32[32,1024]{1,0:T(8,128)S(1)} copy-done((f32[32,1024]{1,0:T(8,128)S(1)}, f32[32,1024]{1,0:T(8,128)}, u32[]{:S(2)}) %copy-start.1) | copy-done | bytes 131096
  2.5 0.0 copy-start.2
  2.5 0.7 %copy-done.2 = f32[3,1,8,128]{3,2,1,0:T(8,128)S(1)} copy-done((f32[3,1,8,128]{3,2,1,0:T(8,128)S(1)}, f32[3,1,8,128]{3,2,1,0:T(8,128)}, u32[]{:S(2)}) %copy-start.2) | copy-done | bytes 12312
  3.2 61.9 %shard_map.58 = (f32[24,128]{1,0:T(8,128)S(1)}, f32[768,128]{1,0:T(8,128)S(1)}, f32[32,1024]{1,0:T(8,128)S(1)}) custom-call(f32[24,128]{1,0:T(8,128)S(1)} %bitcast.11, f32[768,128]{1,0:T(8,128)S(1)} %bitcast.9, f32[32,1024]{1,0:T(8,128)S(1)} %copy-done.1), custom_call_target="tpu_custom_call" | custom-call | tf_op jit(solution)/shard_map/pallas_call | solution.py:489
  65.1 0.6 copy.11
  65.7 0.7 %copy.12 = f32[32,3,1,8,128]{4,3,2,1,0:T(8,128)} copy(f32[32,3,1,8,128]{4,3,2,1,0:T(8,128)S(1)} %bitcast.8) | data formatting | bytes 786432
  66.5 0.7 copy.13
Async XLA Ops:
  0.6 1.0 %copy-start = (f32[32,3,1,8,128]{4,3,2,1,0:T(8,128)S(1)}, f32[32,3,1,8,128]{4,3,2,1,0:T(8,128)}, u32[]{:S(2)}) copy-start(f32[32,3,1,8,128]{4,3,2,1,0:T(8,128)} %param.4) | copy-start | bytes 1179652
  1.6 0.9 %copy-start.1 = (f32[32,1024]{1,0:T(8,128)S(1)}, f32[32,1024]{1,0:T(8,128)}, u32[]{:S(2)}) copy-start(f32[32,1024]{1,0:T(8,128)} %samples_ref.1) | copy-start | bytes 393220
  2.5 0.7 %copy-start.2 = (f32[3,1,8,128]{3,2,1,0:T(8,128)S(1)}, f32[3,1,8,128]{3,2,1,0:T(8,128)}, u32[]{:S(2)}) copy-start(f32[3,1,8,128]{3,2,1,0:T(8,128)} %param.3) | copy-start | bytes 36868

commit v2 on v1

--- a/solution.py
+++ b/solution.py
@@ -150,27 +150,20 @@
             for off in range(1, count)
         ]
 
-    avg_copies = spread(avg_own, avg_y, ay_ss, ay_rs, "gy", iy, gy)
+    avg_copies = spread(avg_own, avg_x, ax_ss, ax_rs, "gx", ix, gx)
 
     halo = []
     halo.append(send(mean_ref, xm.at[768:792], halo_send.at[0], halo_recv.at[0], "gx", x_next))
     halo.append(send(mean_ref, xp.at[768:792], halo_send.at[1], halo_recv.at[1], "gx", x_prev))
-    for c in range(2):
-        rows = slice(c * 384, (c + 1) * 384)
-        s = 2 + 2 * c
-        halo.append(
-            send(modes_ref.at[rows], xm.at[rows], halo_send.at[s], halo_recv.at[s], "gx", x_next)
-        )
-        halo.append(
-            send(
-                modes_ref.at[rows],
-                xp.at[rows],
-                halo_send.at[s + 1],
-                halo_recv.at[s + 1],
-                "gx",
-                x_prev,
+    for c in range(4):
+        rows = slice(c * 192, (c + 1) * 192)
+        for way, (slots, target) in enumerate(((xm, x_next), (xp, x_prev))):
+            i = 2 + 2 * c + way
+            halo.append(
+                send(
+                    modes_ref.at[rows], slots.at[rows], halo_send.at[i], halo_recv.at[i], "gx", target
+                )
             )
-        )
 
     lane = lax.broadcasted_iota(jnp.int32, (ROWS, LANES), 1)
     to_next = jnp.zeros((ROWS, LANES), f32)
@@ -198,10 +191,10 @@
     for copy in avg_copies:
         copy.wait()
     total = avg_own[...]
-    for off in range(1, gy):
-        total = total + avg_y[off]
+    for off in range(1, gx):
+        total = total + avg_x[off]
     avg_mid[...] = total
-    avg_copies = spread(avg_mid, avg_x, ax_ss, ax_rs, "gx", ix, gx)
+    avg_copies = spread(avg_mid, avg_y, ay_ss, ay_rs, "gy", iy, gy)
 
     for copy in edges:
         copy.wait()
@@ -228,8 +221,8 @@
     for copy in avg_copies:
         copy.wait()
     total = avg_mid[...]
-    for off in range(1, gx):
-        total = total + avg_x[off]
+    for off in range(1, gy):
+        total = total + avg_y[off]
     average = jnp.sum(total, axis=1, keepdims=True) / sample_total
     centred[...] = samples_ref[...] - average
 
@@ -297,45 +290,30 @@
             summed = summed + slots[off]
         full[own_rows, :] = summed
 
-    copies = scatter(sb, sr1, s_ss, s_rs)
-    finish_scatter(copies, sb, sr1, s1)
-    copies = spread(s1, sr2, sx_ss, sx_rs, "gx", ix, gx)
-    finish_spread(copies, s1, sr2, sfull)
-    copies = gather(sfull, sg_ss, sg_rs)
-    for copy in copies:
-        copy.wait()
-
-    second = sfull[:, PAIRS:WIDE]
-    inv = inverse(second)
-    folded = dot(inv, sfull[:, 0:PAIRS], top_degree)
-    p_k = lax.broadcasted_iota(jnp.int32, (K, PAIRS), 1)
-    low = p_k < HALF * HALF
-    q = p_k - HALF * HALF
-    k_of = jnp.where(low, p_k & (HALF - 1), q & (K - 1))
-    l_of = jnp.where(low, p_k >> 4, HALF + (q >> 5))
-    row_of = lax.broadcasted_iota(jnp.int32, (K, PAIRS), 0)
-    choose = jnp.where(k_of == row_of, 1.0, 0.0).astype(f32)
-    spread_cov = dot(second[:, 0:K] / sample_total, choose, top_degree)
-    cov_row = jnp.sum(jnp.where(l_of == row_of, spread_cov, 0.0), axis=0, keepdims=True)
-    full_coef = jnp.concatenate([folded, jnp.broadcast_to(cov_row, (HALF, PAIRS))], axis=0)
-    hi, lo = split(full_coef)
-    coef[0:48, :] = hi
-    coef[48:96, :] = lo
-
-    for copy in halo:
-        copy.wait()
-    for e in range(3):
-        for z in range(NZ):
-            j = e * NZ + z
-            cols = slice(z * LANES, (z + 1) * LANES)
-            before = xm[pl.ds(j, K, stride=24), :]
-            after = xp[pl.ds(j, K, stride=24), :]
-            g[0, e, 0:K, cols] = (after - before) * 0.5
-            lap[e, 0:K, cols] = lap[e, 0:K, cols] + (after + before)
-            before = xm[768 + j : 769 + j, :]
-            after = xp[768 + j : 769 + j, :]
-            g[0, e, K:ROWS, cols] = jnp.broadcast_to((after - before) * 0.5, (ROWS - K, LANES))
-            lap[e, K:ROWS, cols] = lap[e, K:ROWS, cols] + (after + before)
+    s_copies = scatter(sb, sr1, s_ss, s_rs)
+
+    def slope_x(rows, count, first, stride):
+        for e in range(3):
+            for z in range(NZ):
+                j = e * NZ + z
+                cols = slice(z * LANES, (z + 1) * LANES)
+                if stride:
+                    source = pl.ds(first + j, count, stride=stride)
+                else:
+                    source = slice(first + j, first + j + 1)
+                before = xm[source, :]
+                after = xp[source, :]
+                g[0, e, rows, cols] = jnp.broadcast_to((after - before) * 0.5, (8, LANES))
+                lap[e, rows, cols] = lap[e, rows, cols] + (after + before)
+
+    def force(rows, factor):
+        for e in range(3):
+            forced = f[0, K : K + 1, :] * g[0, e, rows] + f[0, rows] * g[0, e, K : K + 1, :]
+            for d in range(1, 3):
+                forced = forced + (
+                    f[d, K : K + 1, :] * g[d, e, rows] + f[d, rows] * g[d, e, K : K + 1, :]
+                )
+            lin[e, rows] = viscosity * lap[e, rows] - factor * forced
 
     def advect_low(l, _):
         row = pl.ds(pl.multiple_of(l * HALF, HALF), HALF)
@@ -369,23 +347,38 @@
             bl[e, diag, :] = lo
         return 0
 
-    lax.fori_loop(0, HALF, advect_low, 0)
-    lax.fori_loop(0, HALF, advect_high, 0)
-
-    for e in range(3):
-        forced = f[0, K : K + 1, :] * g[0, e] + f[0] * g[0, e, K : K + 1, :]
-        for d in range(1, 3):
-            forced = forced + f[d, K : K + 1, :] * g[d, e] + f[d] * g[d, e, K : K + 1, :]
-        lin[e, 0:K] = viscosity * lap[e, 0:K] - forced[0:K]
-        lin[e, K:ROWS] = viscosity * lap[e, K:ROWS] - 0.5 * forced[K:ROWS]
-
-    for r in range(PAIRS // 256):
-        rows = slice(r * 256, (r + 1) * 256)
-        value = jnp.zeros((K, 256), f32)
+    def project(start, count):
+        rows = slice(start, start + count)
+        value = jnp.zeros((K, count), f32)
         for e in range(3):
             first = dot_nt(mt[e], bh[e, rows, :])
             value = value + (first[0:K] + first[K : 2 * K] + dot_nt(mt[e, 0:K], bl[e, rows, :]))
         tb[:, rows] = value
+
+    halo[0].wait()
+    halo[1].wait()
+    slope_x(slice(K, ROWS), 1, 768, 0)
+    force(slice(K, ROWS), 0.5)
+    for c in range(4):
+        halo[2 + 2 * c].wait()
+        halo[3 + 2 * c].wait()
+        rows = slice(8 * c, 8 * c + 8)
+        slope_x(rows, 8, 192 * c, 24)
+        force(rows, 1.0)
+        if c < 2:
+            lax.fori_loop(8 * c, 8 * c + 8, advect_low, 0)
+        else:
+            lax.fori_loop(8 * c - HALF, 8 * c - HALF + 8, advect_high, 0)
+        if c == 0:
+            finish_scatter(s_copies, sb, sr1, s1)
+            s_copies = spread(s1, sr2, sx_ss, sx_rs, "gx", ix, gx)
+        if c == 1:
+            project(0, 256)
+        if c >= 2:
+            project(256 * (c - 1), 256)
+        if c == 2:
+            finish_spread(s_copies, s1, sr2, sfull)
+            s_copies = gather(sfull, sg_ss, sg_rs)
     lin_t = jnp.zeros((K, K), f32)
     lin_n = jnp.zeros((K, K), f32)
     for e in range(3):
@@ -397,6 +390,27 @@
     tb[:, PAIRS : PAIRS + K] = lin_t
     tb[:, PAIRS + K : PAIRS + 2 * K] = lin_n
 
+    copies = scatter(tb, tr1, t_ss, t_rs)
+    for copy in s_copies:
+        copy.wait()
+
+    second = sfull[:, PAIRS:WIDE]
+    inv = inverse(second)
+    folded = dot(inv, sfull[:, 0:PAIRS], top_degree)
+    p_k = lax.broadcasted_iota(jnp.int32, (K, PAIRS), 1)
+    low = p_k < HALF * HALF
+    q = p_k - HALF * HALF
+    k_of = jnp.where(low, p_k & (HALF - 1), q & (K - 1))
+    l_of = jnp.where(low, p_k >> 4, HALF + (q >> 5))
+    row_of = lax.broadcasted_iota(jnp.int32, (K, PAIRS), 0)
+    choose = jnp.where(k_of == row_of, 1.0, 0.0).astype(f32)
+    spread_cov = dot(second[:, 0:K] / sample_total, choose, top_degree)
+    cov_row = jnp.sum(jnp.where(l_of == row_of, spread_cov, 0.0), axis=0, keepdims=True)
+    full_coef = jnp.concatenate([folded, jnp.broadcast_to(cov_row, (HALF, PAIRS))], axis=0)
+    hi, lo = split(full_coef)
+    coef[0:48, :] = hi
+    coef[48:96, :] = lo
+
     def tendency(e):
         def step(i, _):
             cols = pl.ds(pl.multiple_of(i * 256, 256), 256)
@@ -407,13 +421,12 @@
 
         lax.fori_loop(0, CELLS // 256, step, 0)
 
-    copies = scatter(tb, tr1, t_ss, t_rs)
-    tendency(0)
     finish_scatter(copies, tb, tr1, t1)
     copies = spread(t1, tr2, tx_ss, tx_rs, "gx", ix, gx)
-    tendency(1)
+    tendency(0)
     finish_spread(copies, t1, tr2, tfull)
     copies = gather(tfull, tg_ss, tg_rs)
+    tendency(1)
     tendency(2)
     for e in range(3):
         for z in range(NZ):
@@ -483,7 +496,7 @@
             pltpu.VMEM((gx, 8, WIDE), f32),
             pltpu.VMEM((K, WIDE), f32),
         ]
-    sems = [dma(6), dma(6), dma(2), dma(2), dma(gy), dma(gy), dma(gx), dma(gx)]
+    sems = [dma(10), dma(10), dma(2), dma(2), dma(gy), dma(gy), dma(gx), dma(gx)]
     for _ in range(2):
         sems += [dma(gy), dma(gy), dma(gx), dma(gx), dma(gy), dma(gy)]
     mean_rate, modes_rate, sample_rate = pl.pallas_call(

time: 67.4 us -> 49 us (0.73)
  Pallas kernels: 61.9 us -> 43.6 us
    pallas_call x1, Pallas kernels: 61.9 us -> 43.6 us  [body(): pl.pallas_call(functools.partial(kernel, gx, gy), out_shape=(jax.ShapeDty...]
where the time goes in v2:
time: 49 us; the launch traced here: 48.8 us
  Pallas kernels  43.6 us (89%)
  local copies, waits for them, and re-layouts  4.6 us (9%)
  between operations  0.65 us (1%)
    pallas_call x1, Pallas kernels, body(): pl.pallas_call(functools.partial(kernel, gx, gy), out_shape=(jax.ShapeDty...  43.6 us
    unnamed x9, local copies, waits for them, and re-layouts  4.6 us

profile of v2, /device:TPU:0, one launch (start us, length us, event | category | flops | bytes accessed | tf_op | source)
XLA Modules:
  0.0 48.8 jit_solution(15020830974213171009)
XLA Ops:
  0.6 0.0 copy-start
  0.6 1.0 %copy-done = f32[32,3,1,8,128]{4,3,2,1,0:T(8,128)S(1)} copy-done((f32[32,3,1,8,128]{4,3,2,1,0:T(8,128)S(1)}, f32[32,3,1,8,128]{4,3,2,1,0:T(8,128)}, u32[]{:S(2)}) %copy-start) | copy-done | bytes 393240
  1.6 0.0 copy-start.1
  1.6 0.9 %copy-done.1 = f32[32,1024]{1,0:T(8,128)S(1)} copy-done((f32[32,1024]{1,0:T(8,128)S(1)}, f32[32,1024]{1,0:T(8,128)}, u32[]{:S(2)}) %copy-start.1) | copy-done | bytes 131096
  2.5 0.0 copy-start.2
  2.5 0.7 %copy-done.2 = f32[3,1,8,128]{3,2,1,0:T(8,128)S(1)} copy-done((f32[3,1,8,128]{3,2,1,0:T(8,128)S(1)}, f32[3,1,8,128]{3,2,1,0:T(8,128)}, u32[]{:S(2)}) %copy-start.2) | copy-done | bytes 12312
  3.2 43.6 %shard_map.58 = (f32[24,128]{1,0:T(8,128)S(1)}, f32[768,128]{1,0:T(8,128)S(1)}, f32[32,1024]{1,0:T(8,128)S(1)}) custom-call(f32[24,128]{1,0:T(8,128)S(1)} %bitcast.11, f32[768,128]{1,0:T(8,128)S(1)} %bitcast.9, f32[32,1024]{1,0:T(8,128)S(1)} %copy-done.1), custom_call_target="tpu_custom_call" | custom-call | tf_op jit(solution)/shard_map/pallas_call | solution.py:502
  46.8 0.6 %copy.11 = f32[3,1,8,128]{3,2,1,0:T(8,128)} copy(f32[3,1,8,128]{3,2,1,0:T(8,128)S(1)} %bitcast.10) | data formatting | bytes 24576
  47.4 0.7 %copy.12 = f32[32,3,1,8,128]{4,3,2,1,0:T(8,128)} copy(f32[32,3,1,8,128]{4,3,2,1,0:T(8,128)S(1)} %bitcast.8) | data formatting | bytes 786432
  48.2 0.7 %copy.13 = f32[32,1024]{1,0:T(8,128)} copy(f32[32,1024]{1,0:T(8,128)S(1)} %get-tuple-element.17) | data formatting | bytes 262144
Async XLA Ops:
  0.6 1.0 %copy-start = (f32[32,3,1,8,128]{4,3,2,1,0:T(8,128)S(1)}, f32[32,3,1,8,128]{4,3,2,1,0:T(8,128)}, u32[]{:S(2)}) copy-start(f32[32,3,1,8,128]{4,3,2,1,0:T(8,128)} %param.4) | copy-start | bytes 1179652
  1.6 0.9 %copy-start.1 = (f32[32,1024]{1,0:T(8,128)S(1)}, f32[32,1024]{1,0:T(8,128)}, u32[]{:S(2)}) copy-start(f32[32,1024]{1,0:T(8,128)} %samples_ref.1) | copy-start | bytes 393220
  2.5 0.7 %copy-start.2 = (f32[3,1,8,128]{3,2,1,0:T(8,128)S(1)}, f32[3,1,8,128]{3,2,1,0:T(8,128)}, u32[]{:S(2)}) copy-start(f32[3,1,8,128]{3,2,1,0:T(8,128)} %param.3) | copy-start | bytes 36868

commit v3 on v2

--- a/solution.py
+++ b/solution.py
@@ -17,8 +17,10 @@
 NZ = 8
 LANES = 128
 CELLS = NZ * LANES
+EARLY = 512
 PAIRS = HALF * HALF + HALF * K
 WIDE = PAIRS + LANES
+LATE = WIDE - EARLY
 ROWS = 40
 
 
@@ -82,6 +84,11 @@
     s1,
     sr2,
     sfull,
+    ub,
+    ur1,
+    u1,
+    ur2,
+    ufull,
     tb,
     tr1,
     t1,
@@ -101,6 +108,12 @@
     sx_rs,
     sg_ss,
     sg_rs,
+    u_ss,
+    u_rs,
+    ux_ss,
+    ux_rs,
+    ug_ss,
+    ug_rs,
     t_ss,
     t_rs,
     tx_ss,
@@ -155,8 +168,12 @@
     halo = []
     halo.append(send(mean_ref, xm.at[768:792], halo_send.at[0], halo_recv.at[0], "gx", x_next))
     halo.append(send(mean_ref, xp.at[768:792], halo_send.at[1], halo_recv.at[1], "gx", x_prev))
-    for c in range(4):
+
+    def send_chunk(c):
         rows = slice(c * 192, (c + 1) * 192)
+        if c >= 2:
+            halo[2 * c - 2].wait_send()
+            halo[2 * c - 1].wait_send()
         for way, (slots, target) in enumerate(((xm, x_next), (xp, x_prev))):
             i = 2 + 2 * c + way
             halo.append(
@@ -164,6 +181,9 @@
                     modes_ref.at[rows], slots.at[rows], halo_send.at[i], halo_recv.at[i], "gx", target
                 )
             )
+
+    send_chunk(0)
+    send_chunk(1)
 
     lane = lax.broadcasted_iota(jnp.int32, (ROWS, LANES), 1)
     to_next = jnp.zeros((ROWS, LANES), f32)
@@ -218,80 +238,6 @@
             g[2, e, :, cols] = (above - below) * 0.5
             lap[e, :, cols] = after + before + above + below - 6.0 * piece
 
-    for copy in avg_copies:
-        copy.wait()
-    total = avg_mid[...]
-    for off in range(1, gy):
-        total = total + avg_y[off]
-    average = jnp.sum(total, axis=1, keepdims=True) / sample_total
-    centred[...] = samples_ref[...] - average
-
-    def pair_low(l, _):
-        row = pl.ds(pl.multiple_of(l * HALF, HALF), HALF)
-        hi, lo = split(centred[0:HALF, :] * centred[pl.ds(l, 1), :])
-        ph[row, :] = hi
-        plo[row, :] = lo
-        return 0
-
-    def pair_high(l, _):
-        row = pl.ds(pl.multiple_of(HALF * HALF + l * K, HALF), K)
-        hi, lo = split(centred[...] * centred[pl.ds(l + HALF, 1), :])
-        ph[row, :] = hi
-        plo[row, :] = lo
-        return 0
-
-    lax.fori_loop(0, HALF, pair_low, 0)
-    lax.fori_loop(0, HALF, pair_high, 0)
-    c_hi, c_lo = split(centred[...])
-    c_both = jnp.concatenate([c_hi, c_lo], axis=0)
-    for r in range(PAIRS // 256):
-        rows = slice(r * 256, (r + 1) * 256)
-        first = dot_nt(c_both, ph[rows, :])
-        sb[:, rows] = first[0:K] + first[K : 2 * K] + dot_nt(c_hi, plo[rows, :])
-    sb[:, PAIRS:WIDE] = jnp.zeros((K, LANES), f32)
-    sb[:, PAIRS : PAIRS + K] = dot_nt(centred[...], centred[...], top_degree)
-
-    own_rows = pl.ds(pl.multiple_of(iy * 8, 8), 8)
-
-    def scatter(src, slots, ss, rs):
-        copies = []
-        for off in range(1, gy):
-            target = lax.rem(iy + off, gy)
-            rows = pl.ds(pl.multiple_of(target * 8, 8), 8)
-            copies.append(send(src.at[rows], slots.at[off], ss.at[off], rs.at[off], "gy", target))
-        return copies
-
-    def gather(full, ss, rs):
-        return [
-            send(
-                full.at[own_rows],
-                full.at[own_rows],
-                ss.at[off],
-                rs.at[off],
-                "gy",
-                lax.rem(iy + off, gy),
-            )
-            for off in range(1, gy)
-        ]
-
-    def finish_scatter(copies, src, slots, out):
-        for copy in copies:
-            copy.wait()
-        summed = src[own_rows, :]
-        for off in range(1, gy):
-            summed = summed + slots[off]
-        out[...] = summed
-
-    def finish_spread(copies, own, slots, full):
-        for copy in copies:
-            copy.wait()
-        summed = own[...]
-        for off in range(1, gx):
-            summed = summed + slots[off]
-        full[own_rows, :] = summed
-
-    s_copies = scatter(sb, sr1, s_ss, s_rs)
-
     def slope_x(rows, count, first, stride):
         for e in range(3):
             for z in range(NZ):
@@ -349,19 +295,21 @@
 
     def project(start, count):
         rows = slice(start, start + count)
-        value = jnp.zeros((K, count), f32)
+        first = jnp.zeros((count, 2 * K), f32)
+        second = jnp.zeros((count, K), f32)
         for e in range(3):
-            first = dot_nt(mt[e], bh[e, rows, :])
-            value = value + (first[0:K] + first[K : 2 * K] + dot_nt(mt[e, 0:K], bl[e, rows, :]))
-        tb[:, rows] = value
-
-    halo[0].wait()
-    halo[1].wait()
-    slope_x(slice(K, ROWS), 1, 768, 0)
-    force(slice(K, ROWS), 0.5)
-    for c in range(4):
-        halo[2 + 2 * c].wait()
-        halo[3 + 2 * c].wait()
+            first = first + dot_nt(bh[e, rows, :], mt[e])
+            second = second + dot_nt(bl[e, rows, :], mt[e, 0:K])
+        first = first.T
+        value = first[0:K] + first[K : 2 * K] + second.T
+        if start < EARLY:
+            ub[:, rows] = value
+        else:
+            tb[:, start - EARLY : start - EARLY + count] = value
+
+    def work(c):
+        halo[2 + 2 * c].wait_recv()
+        halo[3 + 2 * c].wait_recv()
         rows = slice(8 * c, 8 * c + 8)
         slope_x(rows, 8, 192 * c, 24)
         force(rows, 1.0)
@@ -369,16 +317,106 @@
             lax.fori_loop(8 * c, 8 * c + 8, advect_low, 0)
         else:
             lax.fori_loop(8 * c - HALF, 8 * c - HALF + 8, advect_high, 0)
-        if c == 0:
-            finish_scatter(s_copies, sb, sr1, s1)
-            s_copies = spread(s1, sr2, sx_ss, sx_rs, "gx", ix, gx)
-        if c == 1:
-            project(0, 256)
-        if c >= 2:
-            project(256 * (c - 1), 256)
-        if c == 2:
-            finish_spread(s_copies, s1, sr2, sfull)
-            s_copies = gather(sfull, sg_ss, sg_rs)
+
+    send_chunk(2)
+    halo[0].wait()
+    halo[1].wait()
+    slope_x(slice(K, ROWS), 1, 768, 0)
+    force(slice(K, ROWS), 0.5)
+    work(0)
+
+    for copy in avg_copies:
+        copy.wait()
+    total = avg_mid[...]
+    for off in range(1, gy):
+        total = total + avg_y[off]
+    average = jnp.sum(total, axis=1, keepdims=True) / sample_total
+    centred[...] = samples_ref[...] - average
+
+    def pair_low(l, _):
+        row = pl.ds(pl.multiple_of(l * HALF, HALF), HALF)
+        hi, lo = split(centred[0:HALF, :] * centred[pl.ds(l, 1), :])
+        ph[row, :] = hi
+        plo[row, :] = lo
+        return 0
+
+    def pair_high(l, _):
+        row = pl.ds(pl.multiple_of(HALF * HALF + l * K, HALF), K)
+        hi, lo = split(centred[...] * centred[pl.ds(l + HALF, 1), :])
+        ph[row, :] = hi
+        plo[row, :] = lo
+        return 0
+
+    lax.fori_loop(0, HALF, pair_low, 0)
+    lax.fori_loop(0, HALF, pair_high, 0)
+    c_hi, c_lo = split(centred[...])
+    c_both = jnp.concatenate([c_hi, c_lo], axis=0)
+    for r in range(PAIRS // 256):
+        rows = slice(r * 256, (r + 1) * 256)
+        first = dot_nt(c_both, ph[rows, :])
+        sb[:, rows] = first[0:K] + first[K : 2 * K] + dot_nt(c_hi, plo[rows, :])
+    sb[:, PAIRS:WIDE] = jnp.zeros((K, LANES), f32)
+    sb[:, PAIRS : PAIRS + K] = dot_nt(centred[...], centred[...], top_degree)
+
+    own_rows = pl.ds(pl.multiple_of(iy * 8, 8), 8)
+
+    def scatter(src, slots, ss, rs):
+        copies = []
+        for off in range(1, gy):
+            target = lax.rem(iy + off, gy)
+            rows = pl.ds(pl.multiple_of(target * 8, 8), 8)
+            copies.append(send(src.at[rows], slots.at[off], ss.at[off], rs.at[off], "gy", target))
+        return copies
+
+    def gather(full, ss, rs):
+        return [
+            send(
+                full.at[own_rows],
+                full.at[own_rows],
+                ss.at[off],
+                rs.at[off],
+                "gy",
+                lax.rem(iy + off, gy),
+            )
+            for off in range(1, gy)
+        ]
+
+    def finish_scatter(copies, src, slots, out):
+        for copy in copies:
+            copy.wait()
+        summed = src[own_rows, :]
+        for off in range(1, gy):
+            summed = summed + slots[off]
+        out[...] = summed
+
+    def finish_spread(copies, own, slots, full):
+        for copy in copies:
+            copy.wait()
+        summed = own[...]
+        for off in range(1, gx):
+            summed = summed + slots[off]
+        full[own_rows, :] = summed
+
+    s_copies = scatter(sb, sr1, s_ss, s_rs)
+
+    send_chunk(3)
+    work(1)
+    project(0, 256)
+    finish_scatter(s_copies, sb, sr1, s1)
+    s_copies = spread(s1, sr2, sx_ss, sx_rs, "gx", ix, gx)
+    work(2)
+    project(256, 256)
+    u_copies = scatter(ub, ur1, u_ss, u_rs)
+    finish_spread(s_copies, s1, sr2, sfull)
+    s_copies = gather(sfull, sg_ss, sg_rs)
+    work(3)
+    finish_scatter(u_copies, ub, ur1, u1)
+    u_copies = spread(u1, ur2, ux_ss, ux_rs, "gx", ix, gx)
+    project(512, 256)
+    halo[8].wait_send()
+    halo[9].wait_send()
+    halo[6].wait_send()
+    halo[7].wait_send()
     lin_t = jnp.zeros((K, K), f32)
     lin_n = jnp.zeros((K, K), f32)
     for e in range(3):
@@ -386,11 +424,16 @@
         m_hi, m_lo = mt[e, 0:K], mt[e, K : 2 * K]
         lin_t = lin_t + (dot_nt(m_hi, lin_hi) + dot_nt(m_lo, lin_hi) + dot_nt(m_hi, lin_lo))
         lin_n = lin_n + (dot_nt(lin_hi, m_hi) + dot_nt(lin_hi, m_lo) + dot_nt(lin_lo, m_hi))
-    tb[:, PAIRS:WIDE] = jnp.zeros((K, LANES), f32)
-    tb[:, PAIRS : PAIRS + K] = lin_t
-    tb[:, PAIRS + K : PAIRS + 2 * K] = lin_n
+    tb[:, PAIRS - EARLY : LATE] = jnp.zeros((K, LANES), f32)
+    ends_at = PAIRS - EARLY
+    tb[:, ends_at : ends_at + K] = lin_t
+    tb[:, ends_at + K : ends_at + 2 * K] = lin_n
 
     copies = scatter(tb, tr1, t_ss, t_rs)
+    finish_spread(u_copies, u1, ur2, ufull)
+    u_copies = gather(ufull, ug_ss, ug_rs)
+    finish_scatter(copies, tb, tr1, t1)
+    copies = spread(t1, tr2, tx_ss, tx_rs, "gx", ix, gx)
     for copy in s_copies:
         copy.wait()
 
@@ -421,8 +464,6 @@
 
         lax.fori_loop(0, CELLS // 256, step, 0)
 
-    finish_scatter(copies, tb, tr1, t1)
-    copies = spread(t1, tr2, tx_ss, tx_rs, "gx", ix, gx)
     tendency(0)
     finish_spread(copies, t1, tr2, tfull)
     copies = gather(tfull, tg_ss, tg_rs)
@@ -435,8 +476,10 @@
     for copy in copies:
         copy.wait()
 
-    triple = tfull[:, 0:PAIRS] / total_cells
-    ends = tfull[:, PAIRS:WIDE] / total_cells
+    for copy in u_copies:
+        copy.wait()
+    triple = jnp.concatenate([ufull[...], tfull[:, 0:ends_at]], axis=1) / total_cells
+    ends = tfull[:, ends_at:LATE] / total_cells
     tangent = ends[:, K : 2 * K] - dot_nt(full_coef[0:K], triple, top_degree)
     a_hi, a_lo = split(tangent)
     a_both = jnp.concatenate([a_hi, a_lo], axis=0)
@@ -488,16 +531,16 @@
         pltpu.VMEM((2, ROWS, LANES), f32),
         pltpu.VMEM((2, ROWS, LANES), f32),
     ]
-    for _ in range(2):
+    for width in (WIDE, EARLY, LATE):
         scratch += [
-            pltpu.VMEM((K, WIDE), f32),
-            pltpu.VMEM((gy, 8, WIDE), f32),
-            pltpu.VMEM((8, WIDE), f32),
-            pltpu.VMEM((gx, 8, WIDE), f32),
-            pltpu.VMEM((K, WIDE), f32),
+            pltpu.VMEM((K, width), f32),
+            pltpu.VMEM((gy, 8, width), f32),
+            pltpu.VMEM((8, width), f32),
+            pltpu.VMEM((gx, 8, width), f32),
+            pltpu.VMEM((K, width), f32),
         ]
     sems = [dma(10), dma(10), dma(2), dma(2), dma(gy), dma(gy), dma(gx), dma(gx)]
-    for _ in range(2):
+    for _ in range(3):
         sems += [dma(gy), dma(gy), dma(gx), dma(gx), dma(gy), dma(gy)]
     mean_rate, modes_rate, sample_rate = pl.pallas_call(
         functools.partial(kernel, gx, gy),

time: 49 us -> 48.3 us (0.986)
  Pallas kernels: 43.6 us -> 42.8 us
    pallas_call x1, Pallas kernels: 43.6 us -> 42.8 us  [body(): pl.pallas_call(functools.partial(kernel, gx, gy), out_shape=(jax.ShapeDty...]
where the time goes in v3:
time: 48.3 us; the launch traced here: 48 us
  Pallas kernels  42.8 us (89%)
  local copies, waits for them, and re-layouts  4.6 us (10%)
  between operations  0.65 us (1%)
    pallas_call x1, Pallas kernels, body(): pl.pallas_call(functools.partial(kernel, gx, gy), out_shape=(jax.ShapeDty...  42.8 us
    unnamed x9, local copies, waits for them, and re-layouts  4.6 us

profile of v3, /device:TPU:0, one launch (start us, length us, event | category | flops | bytes accessed | tf_op | source)
XLA Modules:
  0.0 48.0 jit_solution(11855980061339392418)
XLA Ops:
  0.6 0.0 copy-start
  0.6 1.0 %copy-done = f32[32,3,1,8,128]{4,3,2,1,0:T(8,128)S(1)} copy-done((f32[32,3,1,8,128]{4,3,2,1,0:T(8,128)S(1)}, f32[32,3,1,8,128]{4,3,2,1,0:T(8,128)}, u32[]{:S(2)}) %copy-start) | copy-done | bytes 393240
  1.6 0.0 copy-start.1
  1.6 0.9 %copy-done.1 = f32[32,1024]{1,0:T(8,128)S(1)} copy-done((f32[32,1024]{1,0:T(8,128)S(1)}, f32[32,1024]{1,0:T(8,128)}, u32[]{:S(2)}) %copy-start.1) | copy-done | bytes 131096
  2.5 0.0 copy-start.2
  2.5 0.7 %copy-done.2 = f32[3,1,8,128]{3,2,1,0:T(8,128)S(1)} copy-done((f32[3,1,8,128]{3,2,1,0:T(8,128)S(1)}, f32[3,1,8,128]{3,2,1,0:T(8,128)}, u32[]{:S(2)}) %copy-start.2) | copy-done | bytes 12312
  3.2 42.8 %shard_map.58 = (f32[24,128]{1,0:T(8,128)S(1)}, f32[768,128]{1,0:T(8,128)S(1)}, f32[32,1024]{1,0:T(8,128)S(1)}) custom-call(f32[24,128]{1,0:T(8,128)S(1)} %bitcast.11, f32[768,128]{1,0:T(8,128)S(1)} %bitcast.9, f32[32,1024]{1,0:T(8,128)S(1)} %copy-done.1), custom_call_target="tpu_custom_call" | custom-call | tf_op jit(solution)/shard_map/pallas_call | solution.py:545
  46.0 0.6 %copy.11 = f32[3,1,8,128]{3,2,1,0:T(8,128)} copy(f32[3,1,8,128]{3,2,1,0:T(8,128)S(1)} %bitcast.10) | data formatting | bytes 24576
  46.6 0.7 %copy.12 = f32[32,3,1,8,128]{4,3,2,1,0:T(8,128)} copy(f32[32,3,1,8,128]{4,3,2,1,0:T(8,128)S(1)} %bitcast.8) | data formatting | bytes 786432
  47.4 0.7 %copy.13 = f32[32,1024]{1,0:T(8,128)} copy(f32[32,1024]{1,0:T(8,128)S(1)} %get-tuple-element.17) | data formatting | bytes 262144
Async XLA Ops:
  0.6 1.0 %copy-start = (f32[32,3,1,8,128]{4,3,2,1,0:T(8,128)S(1)}, f32[32,3,1,8,128]{4,3,2,1,0:T(8,128)}, u32[]{:S(2)}) copy-start(f32[32,3,1,8,128]{4,3,2,1,0:T(8,128)} %param.4) | copy-start | bytes 1179652
  1.6 0.9 %copy-start.1 = (f32[32,1024]{1,0:T(8,128)S(1)}, f32[32,1024]{1,0:T(8,128)}, u32[]{:S(2)}) copy-start(f32[32,1024]{1,0:T(8,128)} %samples_ref.1) | copy-start | bytes 393220
  2.5 0.7 %copy-start.2 = (f32[3,1,8,128]{3,2,1,0:T(8,128)S(1)}, f32[3,1,8,128]{3,2,1,0:T(8,128)}, u32[]{:S(2)}) copy-start(f32[3,1,8,128]{3,2,1,0:T(8,128)} %param.3) | copy-start | bytes 36868

commit v4 on v3

--- a/solution.py
+++ b/solution.py
@@ -171,9 +171,6 @@
 
     def send_chunk(c):
         rows = slice(c * 192, (c + 1) * 192)
-        if c >= 2:
-            halo[2 * c - 2].wait_send()
-            halo[2 * c - 1].wait_send()
         for way, (slots, target) in enumerate(((xm, x_next), (xp, x_prev))):
             i = 2 + 2 * c + way
             halo.append(
@@ -182,8 +179,8 @@
                 )
             )
 
-    send_chunk(0)
-    send_chunk(1)
+    for c in range(4):
+        send_chunk(c)
 
     lane = lax.broadcasted_iota(jnp.int32, (ROWS, LANES), 1)
     to_next = jnp.zeros((ROWS, LANES), f32)
@@ -318,7 +315,6 @@
         else:
             lax.fori_loop(8 * c - HALF, 8 * c - HALF + 8, advect_high, 0)
 
-    send_chunk(2)
     halo[0].wait()
     halo[1].wait()
     slope_x(slice(K, ROWS), 1, 768, 0)
@@ -399,7 +395,6 @@
 
     s_copies = scatter(sb, sr1, s_ss, s_rs)
 
-    send_chunk(3)
     work(1)
     project(0, 256)
     finish_scatter(s_copies, sb, sr1, s1)
@@ -413,10 +408,8 @@
     finish_scatter(u_copies, ub, ur1, u1)
     u_copies = spread(u1, ur2, ux_ss, ux_rs, "gx", ix, gx)
     project(512, 256)
-    halo[8].wait_send()
-    halo[9].wait_send()
-    halo[6].wait_send()
-    halo[7].wait_send()
+    for copy in halo[2:]:
+        copy.wait_send()
     lin_t = jnp.zeros((K, K), f32)
     lin_n = jnp.zeros((K, K), f32)
     for e in range(3):

time: 48.3 us -> 48.3 us (level)
  no operation moved by 1% of the time
where the time goes in v4:
time: 48.3 us; the launch traced here: 48 us
  Pallas kernels  42.8 us (89%)
  local copies, waits for them, and re-layouts  4.6 us (10%)
  between operations  0.65 us (1%)
    pallas_call x1, Pallas kernels, body(): pl.pallas_call(functools.partial(kernel, gx, gy), out_shape=(jax.ShapeDty...  42.8 us
    unnamed x9, local copies, waits for them, and re-layouts  4.6 us

profile of v4, /device:TPU:0, one launch (start us, length us, event | category | flops | bytes accessed | tf_op | source)
XLA Modules:
  0.0 48.0 jit_solution(634475228388391097)
XLA Ops:
  0.6 0.0 copy-start
  0.6 1.0 %copy-done = f32[32,3,1,8,128]{4,3,2,1,0:T(8,128)S(1)} copy-done((f32[32,3,1,8,128]{4,3,2,1,0:T(8,128)S(1)}, f32[32,3,1,8,128]{4,3,2,1,0:T(8,128)}, u32[]{:S(2)}) %copy-start) | copy-done | bytes 393240
  1.6 0.0 copy-start.1
  1.6 0.9 %copy-done.1 = f32[32,1024]{1,0:T(8,128)S(1)} copy-done((f32[32,1024]{1,0:T(8,128)S(1)}, f32[32,1024]{1,0:T(8,128)}, u32[]{:S(2)}) %copy-start.1) | copy-done | bytes 131096
  2.5 0.0 copy-start.2
  2.5 0.7 %copy-done.2 = f32[3,1,8,128]{3,2,1,0:T(8,128)S(1)} copy-done((f32[3,1,8,128]{3,2,1,0:T(8,128)S(1)}, f32[3,1,8,128]{3,2,1,0:T(8,128)}, u32[]{:S(2)}) %copy-start.2) | copy-done | bytes 12312
  3.2 42.8 %shard_map.58 = (f32[24,128]{1,0:T(8,128)S(1)}, f32[768,128]{1,0:T(8,128)S(1)}, f32[32,1024]{1,0:T(8,128)S(1)}) custom-call(f32[24,128]{1,0:T(8,128)S(1)} %bitcast.11, f32[768,128]{1,0:T(8,128)S(1)} %bitcast.9, f32[32,1024]{1,0:T(8,128)S(1)} %copy-done.1), custom_call_target="tpu_custom_call" | custom-call | tf_op jit(solution)/shard_map/pallas_call | solution.py:538
  46.0 0.6 %copy.11 = f32[3,1,8,128]{3,2,1,0:T(8,128)} copy(f32[3,1,8,128]{3,2,1,0:T(8,128)S(1)} %bitcast.10) | data formatting | bytes 24576
  46.6 0.7 %copy.12 = f32[32,3,1,8,128]{4,3,2,1,0:T(8,128)} copy(f32[32,3,1,8,128]{4,3,2,1,0:T(8,128)S(1)} %bitcast.8) | data formatting | bytes 786432
  47.4 0.7 %copy.13 = f32[32,1024]{1,0:T(8,128)} copy(f32[32,1024]{1,0:T(8,128)S(1)} %get-tuple-element.17) | data formatting | bytes 262144
Async XLA Ops:
  0.6 1.0 %copy-start = (f32[32,3,1,8,128]{4,3,2,1,0:T(8,128)S(1)}, f32[32,3,1,8,128]{4,3,2,1,0:T(8,128)}, u32[]{:S(2)}) copy-start(f32[32,3,1,8,128]{4,3,2,1,0:T(8,128)} %param.4) | copy-start | bytes 1179652
  1.6 0.9 %copy-start.1 = (f32[32,1024]{1,0:T(8,128)S(1)}, f32[32,1024]{1,0:T(8,128)}, u32[]{:S(2)}) copy-start(f32[32,1024]{1,0:T(8,128)} %samples_ref.1) | copy-start | bytes 393220
  2.5 0.7 %copy-start.2 = (f32[3,1,8,128]{3,2,1,0:T(8,128)S(1)}, f32[3,1,8,128]{3,2,1,0:T(8,128)}, u32[]{:S(2)}) copy-start(f32[3,1,8,128]{3,2,1,0:T(8,128)} %param.3) | copy-start | bytes 36868
